TPU v7x, 256 devices: a whole 4x4x8 slice. The times are simulated.
256 devices in a mesh: range: 16 (over z, y_lo), blk: 16 (over y_hi, x, core).
Axes of the slice: x: 4, y: 4 (y_hi: 2, y_lo: 2; y = y_hi * 2 + y_lo), z: 8, core: 2. Of those that a mesh axis runs over, the one named last changes fastest.
Arguments:
- queries: bfloat16 [8192, 2048], P(('range', 'blk')), may hold values from -6 to 6
- routing: int32 [8192, 1], P(('range', 'blk')), may hold values from 0 to 15; in each aligned block of 32 rows (0 to 31, 32 to 63, ...) at most 8 rows name the same one
- windows: int32 [8192, 2], P(('range', 'blk')), may hold values from 0 to 2048, as said below
- shifts: int32 [8], replicated, may hold values from -256 to 256
- library: bfloat16 [32768, 2048], P(('range', 'blk')), may hold values from -6 to 6
Outputs:
- match: float32 [8192, 8], P(('range', 'blk'))
Inputs may be any that keep to these rules, and one draw needn't show every extreme that they name: `windows`: lo < hi; hi - lo lies between 128 and 512, and equals 512 for some query. `routing`: within the queries of one device no range is named more than 8 times; some range is named exactly 8 times.
All inputs are finite; a program needn't handle non-finite values.
Results may differ from a plain program's by a relative error of at most 0.0003.
Values may be sent and summed in bfloat16 or wider, within the bound.
A program may use at most 256 MiB of HBM per device.

v0:
```python
import jax
import jax.numpy as jnp
from jax import lax
from jax.sharding import PartitionSpec as P


def shift_copies(spectra, shifts):
    width = spectra.shape[1]
    position = jnp.arange(width, dtype=jnp.int32)
    copies = []
    for offset in range(shifts.shape[0]):
        amount = shifts[offset]
        rolled = jnp.roll(spectra, amount, axis=1)
        source = position - amount
        keep = (source >= 0) & (source < width)
        copies.append(jnp.where(keep[None, :], rolled, jnp.zeros_like(rolled)))
    return jnp.stack(copies, 0)


def window_terms(copies, block, lower, upper):
    width = copies.shape[2]
    scores = lax.dot_general(
        copies, block, (((2,), (1,)), ((), ())), preferred_element_type=jnp.float32
    )
    index = jnp.arange(block.shape[0], dtype=jnp.int32)
    keep = (index[None, :] >= lower[:, None]) & (index[None, :] < upper[:, None])
    level = jnp.maximum(scores * jnp.float32(width) ** (-0.5), 0.0)
    return jnp.sum(jnp.where(keep[None], level * level, 0.0), axis=2)


def local(queries, routing, windows, shifts, library):
    n_range = lax.axis_size("range")
    q_count = queries.shape[0]
    per_range = q_count // 4
    width = queries.shape[1]
    n_offsets = shifts.shape[0]
    slots = n_range * per_range
    target = routing[:, 0]
    onehot = (target[:, None] == jnp.arange(n_range, dtype=jnp.int32)[None, :]).astype(jnp.int32)
    before = jnp.cumsum(onehot, axis=0) - onehot
    place = jnp.sum(before * onehot, axis=1)
    slot_of = target * per_range + place
    table = slot_of[None, :] == jnp.arange(slots, dtype=jnp.int32)[:, None]
    outgoing = jnp.dot(
        table.astype(jnp.bfloat16), queries, preferred_element_type=jnp.float32
    ).astype(jnp.bfloat16)
    filled = jnp.sum(table.astype(jnp.int32), axis=1)
    lower_out = jnp.sum(jnp.where(table, windows[None, :, 0], 0), axis=1)
    upper_out = jnp.sum(jnp.where(table, windows[None, :, 1], 0), axis=1) + (1 - filled)
    bounds = jnp.stack([lower_out, upper_out], axis=1)
    arrived = lax.all_to_all(
        outgoing.reshape(n_range, per_range, width),
        "range",
        split_axis=0,
        concat_axis=0,
        tiled=True,
    ).reshape(slots, width)
    limits = lax.all_to_all(
        bounds.reshape(n_range, per_range, 2), "range", split_axis=0, concat_axis=0, tiled=True
    ).reshape(slots, 2)
    lower = limits[:, 0]
    upper = limits[:, 1]
    spans = (upper - lower).astype(jnp.float32)
    copies = shift_copies(arrived, shifts)
    summed = window_terms(copies, lax.all_gather(library, "blk", axis=0, tiled=True), lower, upper)
    results = (summed / spans[None, :]).T
    returned = lax.all_to_all(
        results.reshape(n_range, per_range, n_offsets),
        "range",
        split_axis=0,
        concat_axis=0,
        tiled=True,
    ).reshape(slots, n_offsets)
    return jnp.dot(
        table.T.astype(jnp.float32),
        returned,
        precision=lax.Precision.HIGHEST,
        preferred_element_type=jnp.float32,
    )


def solution(mesh):
    in_specs = (
        P(("range", "blk"), None),
        P(("range", "blk"), None),
        P(("range", "blk"), None),
        P(),
        P(("range", "blk"), None),
    )
    out_specs = P(("range", "blk"), None)
    return jax.shard_map(local, mesh=mesh, in_specs=in_specs, out_specs=out_specs, check_vma=False)
```

profile of v0, /device:TPU:1, one launch (start us, length us, event | category | flops | bytes accessed | tf_op | source)
XLA Modules:
  0.0 133.2 jit_solution(9433569749145452726)
XLA Ops:
  6.5 0.0 copy-start
  6.5 0.0 all-gather.2.cloned.1.call-start
  6.5 0.7 all-gather.2.cloned.1.call-update
  7.3 0.7 fusion.39
  8.0 0.1 reduce_window_sum.11
  8.0 0.8 select_reduce_fusion.3
  8.9 0.7 multiply_add_fusion
  9.5 0.8 slice_bitcast_fusion.2
  10.3 0.1 select_reduce_fusion.2
  10.4 0.1 add.31
  10.5 0.1 stack.34
  10.6 0.6 copy.10
  11.2 10.1 %all-to-all-start = ((s32[16,8,2]{1,2,0:T(2,128)}), s32[16,8,2]{1,2,0:T(2,128)S(1)}, u32[]{:S(2)}, u32[]{:S(2)}) async-start(s32[16,8,2]{1,2,0:T(2,128)} %copy.10), calls=%async_computation | async-start | bytes 32768 | tf_op jit(solution)/shard_map/all_to_all | solution.py:58
  21.4 1.6 %fusion.66 = (s32[1]{0:T(128)}, s32[1]{0:T(128)}, s32[1]{0:T(128)}, s32[1]{0:T(128)}, s32[1]{0:T(128)}, /*index=5*/s32[1]{0:T(128)}, s32[1]{0:T(128)}, s32[1]{0:T(128)}) fusion(s32[8]{0:T(128)} %param.10), kind=kLoop, calls=%fused_computation.107 | loop fusion | bytes 64 | tf_op jit(solution)/shard_map/slice | solution.py:12
  35.7 0.7 fusion.58
  36.4 0.6 fusion.59
  37.0 0.6 fusion.60
  37.6 0.6 fusion.61
  38.2 0.6 fusion.62
  38.8 0.6 fusion.63
  39.4 0.6 fusion.64
  40.1 0.0 copy-done
  40.1 1.3 fusion.4
  43.3 0.0 all-to-all-done
  43.3 7.6 %all-to-all-start.1 = ((bf16[16,8,2048]{2,1,0:T(8,128)(2,1)}), bf16[16,8,2048]{2,1,0:T(8,128)(2,1)S(1)}, u32[]{:S(2)}, u32[]{:S(2)}) async-start(bf16[16,8,2048]{2,1,0:T(8,128)(2,1)} %fusion.4), calls=%async_computation.1 | async-start | bytes 1048576 | tf_op jit(solution)/shard_map/all_to_all | solution.py:51
  50.9 0.7 fusion.65
  51.6 0.1 reshape.161
  51.7 0.5 fusion.5
  52.2 14.0 %all-to-all-done.1 = bf16[16,8,2048]{2,1,0:T(8,128)(2,1)S(1)} async-done(((bf16[16,8,2048]{2,1,0:T(8,128)(2,1)}), bf16[16,8,2048]{2,1,0:T(8,128)(2,1)S(1)}, u32[]{:S(2)}, u32[]{:S(2)}) %all-to-all-start.1) | async-done | bytes 524320 | tf_op jit(solution)/shard_map/all_to_all | solution.py:51
  66.2 1.3 fusion.13
  67.5 1.3 fusion.17
  68.8 1.3 fusion.21
  70.1 1.3 fusion.25
  71.3 1.3 fusion.29
  72.6 1.3 fusion.33
  73.9 1.3 fusion.37
  75.2 1.3 fusion.9
  76.4 20.7 %all-gather.2.cloned.1.call-done = bf16[2048,2048]{1,0:T(8,128)(2,1)} async-done(((bf16[128,2048]{1,0:T(8,128)(2,1)}), bf16[2048,2048]{1,0:T(8,128)(2,1)}) %all-gather.2.cloned.1.call-update) | async-done | bytes 8388624 | tf_op jit(solution)/shard_map/all_gather | solution.py:65
  97.1 13.2 %select_reduce_fusion = f32[8,128]{1,0:T(8,128)S(1)} fusion(bf16[8,128,2048]{2,1,0:T(8,128)(2,1)} %fusion.9, bf16[2048,2048]{1,0:T(8,128)(2,1)} %all-gather.2.cloned.1.call-done, pred[128,2048]{1,0:T(8,128)(4,1)S(1)} %fusion.5), kind=kOutput, calls=%fused_computation.2 | convolution fusion | flops 8600419328 | bytes 12849152 | tf_op jit(solution)/shard_map/dot_general | solution.py:22
  110.3 0.1 reshape.164
  110.4 15.0 %all_to_all.15 = f32[16,8,8]{1,2,0:T(8,128)S(1)} all-to-all(f32[16,8,8]{1,2,0:T(8,128)S(1)} %copy.12), channel_id=1, replica_groups=mesh['range'=16,'blk'=16] {'range'}, dimensions={0} | all-to-all | bytes 8192 | tf_op jit(solution)/shard_map/all_to_all | solution.py:67
  125.4 0.1 reshape.165
  125.5 0.8 fusion.38
  (8 shorter events, 0.1 us)
Async XLA Ops:
  6.5 33.5 %copy-start = (bf16[32,2048]{1,0:T(8,128)(2,1)S(1)}, bf16[32,2048]{1,0:T(8,128)(2,1)}, u32[]{:S(2)}) copy-start(bf16[32,2048]{1,0:T(8,128)(2,1)} %param.7) | copy-start | bytes 393220
  6.5 90.6 %all-gather.2.cloned.1.call-start = ((), (), s32[]{:S(2)}) async-start(), calls=%async_computation.3 | async-start | bytes 8912896 | tf_op jit(solution)/shard_map/all_gather | solution.py:65
  11.2 32.1 %all-to-all-start = ((s32[16,8,2]{1,2,0:T(2,128)}), s32[16,8,2]{1,2,0:T(2,128)S(1)}, u32[]{:S(2)}, u32[]{:S(2)}) async-start(s32[16,8,2]{1,2,0:T(2,128)} %copy.10), calls=%async_computation | async-start | bytes 32768 | tf_op jit(solution)/shard_map/all_to_all | solution.py:58
  43.3 22.8 %all-to-all-start.1 = ((bf16[16,8,2048]{2,1,0:T(8,128)(2,1)}), bf16[16,8,2048]{2,1,0:T(8,128)(2,1)S(1)}, u32[]{:S(2)}, u32[]{:S(2)}) async-start(bf16[16,8,2048]{2,1,0:T(8,128)(2,1)} %fusion.4), calls=%async_computation.1 | async-start | bytes 1048576 | tf_op jit(solution)/shard_map/all_to_all | solution.py:51
Sparse Core Ops, SparseCore 0:
  10.1 86.9 all-gather.1
where the time goes:
time: 134 us; the launch traced here: 133 us
  waiting for transfers between devices  35.4 us (26%)
  between operations  28.3 us (21%)
  other arithmetic  18.1 us (14%)
  starting transfers between devices  17.7 us (13%)
  matrix products  15.2 us (11%)
  blocking collectives  15 us (11%)
  local copies, waits for them, and re-layouts  3.45 us (3%)
    all_gather x1, waiting for transfers between devices, local(): lax.all_gather(library, 'blk', axis=0, tiled=True)  20.7 us
    all_to_all x1, blocking collectives, local(): lax.all_to_all(results.reshape(n_range, per_range, n_offsets), 'range', s...  15 us
    all_to_all x1, waiting for transfers between devices, local(): lax.all_to_all(outgoing.reshape(n_range, per_range, width), 'range', spli...  14 us
    dot_general x1, matrix products, window_terms(): lax.dot_general(copies, block, (((2,), (1,)), ((), ())), preferred_elemen...  13.2 us
    all_to_all x1, starting transfers between devices, local(): lax.all_to_all(bounds.reshape(n_range, per_range, 2), 'range', split_axis...  10.1 us
    unnamed x7, other arithmetic  8.99 us
    all_to_all x1, starting transfers between devices, local(): lax.all_to_all(outgoing.reshape(n_range, per_range, width), 'range', spli...  7.56 us
    and x8, other arithmetic, shift_copies(): keep = (source >= 0) & (source < width)  4.93 us
  transfers between devices with their start and end apart: 3, of which 2 were waited for; matrix products, arithmetic and copies ran while one was open for 17% of the time, Pallas kernels for 0%

commit v1 on v0

v1 whole, which is shorter than its diff:
```python
import functools

import jax
import jax.numpy as jnp
from jax import lax
from jax.experimental import pallas as pl
from jax.experimental.pallas import tpu as pltpu
from jax.sharding import PartitionSpec as P

MESH = pl.DeviceIdType.MESH
LANES = 128
PAD = 256


def column_to_row(column, width, period):
    rows = column.shape[0]
    p = lax.broadcasted_iota(jnp.int32, (rows, width), 0)
    c = lax.broadcasted_iota(jnp.int32, (rows, width), 1)
    same = p == lax.rem(c, period)
    return jnp.sum(jnp.where(same, column, 0.0), axis=0, keepdims=True)


def kernel(
    n_range, n_x, sizes,
    q_ref, routing_ref, windows_ref, shifts_ref, lib_ref, out_ref,
    tx, rx, groups, passing, lt, padded, shifted, weight, res, part, total, ret,
    lib_send, lib_recv, a2a_send, a2a_recv, sib_send, sib_recv, y_send, y_recv,
    part_send, part_recv, ret_send, ret_recv,
):
    q_count, width, cap, lib_dev, n_off = sizes
    half = width // 2
    slots = n_range * cap
    me = lax.axis_index("range")
    blk = lax.axis_index("blk")
    core = lax.rem(blk, 2)
    x = lax.rem(lax.div(blk, 2), n_x)
    yh = lax.div(blk, 2 * n_x)
    z = lax.div(me, 2)
    yl = lax.rem(me, 2)

    def block_of(yh_, x_, core_):
        return yh_ * (2 * n_x) + x_ * 2 + core_

    right = {"blk": block_of(yh, lax.rem(x + 1, n_x), core)}
    left = {"blk": block_of(yh, lax.rem(x + n_x - 1, n_x), core)}
    sibling = {"blk": block_of(yh, x, 1 - core)}
    across = {"blk": block_of(1 - yh, x, core)}
    diagonal = {"blk": block_of(1 - yh, x, 1 - core)}
    y = yh * 2 + yl

    def along_y(step):
        there = lax.rem(y + step, 4)
        return {
            "range": z * 2 + lax.rem(there, 2),
            "blk": block_of(lax.div(there, 2), x, core),
        }

    onward = along_y(1 + 2 * core)
    backward = along_y(3 - 2 * core)

    barrier = pltpu.get_barrier_semaphore()

    def greet(k, carry):
        pl.semaphore_signal(
            barrier, inc=1, device_id={"range": lax.rem(me + k, n_range)}, device_id_type=MESH
        )
        return carry

    lax.fori_loop(1, n_range, greet, 0)
    near = (right, left, sibling, across, diagonal, onward, backward)
    for device in near:
        pl.semaphore_signal(barrier, inc=1, device_id=device, device_id_type=MESH)

    target = routing_ref[...].astype(jnp.float32)
    t_row = column_to_row(target, 2 * q_count, q_count)
    p = lax.broadcasted_iota(jnp.int32, (q_count, 2 * q_count), 0)
    c = lax.broadcasted_iota(jnp.int32, (q_count, 2 * q_count), 1)
    earlier = (target == t_row) & (p < lax.rem(c, q_count))
    slot_row = t_row * cap + jnp.sum(jnp.where(earlier, 1.0, 0.0), axis=0, keepdims=True)
    r = lax.broadcasted_iota(jnp.int32, (2 * slots, 2 * q_count), 0)
    c = lax.broadcasted_iota(jnp.int32, (2 * slots, 2 * q_count), 1)
    r_slot = lax.div(r, 2 * cap) * cap + lax.rem(r, cap)
    r_half = lax.rem(lax.div(r, cap), 2)
    hit = (r_slot.astype(jnp.float32) == slot_row) & (r_half == lax.div(c, q_count))
    table = jnp.where(hit, 1.0, 0.0).astype(jnp.bfloat16)
    stacked = jnp.concatenate([q_ref[:, :half], q_ref[:, half:]], axis=0)
    tx[:, :, :half] = (
        jnp.dot(table, stacked, preferred_element_type=jnp.float32)
        .astype(jnp.bfloat16)
        .reshape(n_range, 2 * cap, half)
    )
    first = windows_ref[:, 0:1]
    last = windows_ref[:, 1:2]
    lane = lax.broadcasted_iota(jnp.int32, (q_count, LANES), 1)
    coded = jnp.where(
        lane == 0, lax.div(first, 64),
        jnp.where(lane == 1, lax.rem(first, 64),
                  jnp.where(lane == 2, lax.div(last, 64),
                            jnp.where(lane == 3, lax.rem(last, 64), 0))))
    coded = coded.astype(jnp.float32).astype(jnp.bfloat16)
    coded = jnp.concatenate([coded, coded], axis=0)
    tx[:, :, half:] = (
        jnp.dot(table, coded, preferred_element_type=jnp.float32)
        .astype(jnp.bfloat16)
        .reshape(n_range, 2 * cap, LANES)
    )
    rx[me] = tx[me]

    pieces = lt.shape[1]
    depth = width // pieces
    for k in range(pieces):
        block = lib_ref[:, k * depth:(k + 1) * depth].astype(jnp.float32).T
        padded[0, PAD + k * depth:PAD + (k + 1) * depth, :] = block
        lt[0, k] = block.astype(jnp.bfloat16)
    for b in range(n_x):
        padded[b, :PAD, :] = jnp.zeros((PAD, LANES), jnp.float32)
        padded[b, PAD + width:, :] = jnp.zeros((PAD, LANES), jnp.float32)

    pl.semaphore_wait(barrier, n_range - 1 + len(near))

    def a2a(k):
        there = lax.rem(me + k, n_range)
        return pltpu.make_async_remote_copy(
            src_ref=tx.at[there], dst_ref=rx.at[me],
            send_sem=a2a_send.at[there], recv_sem=a2a_recv.at[me],
            device_id={"range": there}, device_id_type=MESH,
        )

    def a2a_from(source):
        return pltpu.make_async_remote_copy(
            src_ref=tx.at[source], dst_ref=rx.at[source],
            send_sem=a2a_send.at[source], recv_sem=a2a_recv.at[source],
            device_id={"range": source}, device_id_type=MESH,
        )

    def lib_copy(way, k, source, landing, device):
        return pltpu.make_async_remote_copy(
            src_ref=lt.at[source, k], dst_ref=lt.at[landing, k],
            send_sem=lib_send.at[way, k], recv_sem=lib_recv.at[way, k],
            device_id=device, device_id_type=MESH,
        )

    def start_a2a(k, carry):
        a2a(k).start()
        return carry

    split = pieces // 2
    order = list(range(pieces))
    to_right = {k: lib_copy(0, k, 0, 1, right) for k in order}
    to_left = {k: lib_copy(1, k, 0, 2, left) for k in order}
    on_right = {k: lib_copy(2, k, 1, 3, right) for k in order[:split]}
    on_left = {k: lib_copy(2, k, 2, 3, left) for k in order[split:]}

    for k in order[:split]:
        to_right[k].start()
        to_left[k + split].start()
    lax.fori_loop(1, n_range, start_a2a, 0)
    for k in order[:split]:
        to_right[k + split].start()
        to_left[k].start()

    rows = 256

    def shift_block(b):
        def one(step, carry):
            o = lax.div(step, width // rows)
            at = pl.multiple_of(lax.rem(step, width // rows) * rows, rows)
            moved = padded[b, pl.ds(PAD + shifts_ref[o] + at, rows), :]
            shifted[o, pl.ds(at, rows), b * LANES:(b + 1) * LANES] = moved.astype(jnp.bfloat16)
            return carry

        lax.fori_loop(0, n_off * (width // rows), one, 0)

    def widen(b):
        for k in order:
            padded[b, PAD + k * depth:PAD + (k + 1) * depth, :] = lt[b, k].astype(jnp.float32)

    shift_block(0)

    for k in range(split):
        to_right[k].wait_recv()
        on_right[k].start()
        to_left[k + split].wait_recv()
        on_left[k + split].start()

    subs = groups.shape[1]
    sub_rows = groups.shape[2]
    per_sub = n_range // subs
    pr = lax.broadcasted_iota(jnp.int32, (sub_rows, 2 * sub_rows), 0)
    pc = lax.broadcasted_iota(jnp.int32, (sub_rows, 2 * sub_rows), 1)
    source_row = lax.div(pr, cap) * (2 * cap) + lax.rem(pr, cap)
    pick_low = jnp.where(pc == source_row, 1.0, 0.0).astype(jnp.bfloat16)
    pick_high = jnp.where(pc == source_row + cap, 1.0, 0.0).astype(jnp.bfloat16)

    def sib_copy(way, j, group, landing):
        return pltpu.make_async_remote_copy(
            src_ref=groups.at[group, j], dst_ref=groups.at[landing, j],
            send_sem=sib_send.at[way, j], recv_sem=sib_recv.at[way, j],
            device_id=sibling, device_id_type=MESH,
        )

    def y_first(j):
        return pltpu.make_async_remote_copy(
            src_ref=groups.at[0, j], dst_ref=passing.at[j],
            send_sem=y_send.at[0, j], recv_sem=y_recv.at[0, j],
            device_id=onward, device_id_type=MESH,
        )

    def y_second(j):
        return pltpu.make_async_remote_copy(
            src_ref=passing.at[j], dst_ref=groups.at[2, j],
            send_sem=y_send.at[1, j], recv_sem=y_recv.at[1, j],
            device_id=onward, device_id_type=MESH,
        )

    home = lax.div(me, per_sub)

    def sub_of(k):
        return lax.rem(home + k, subs)

    def gather_sub(k, carry):
        j = sub_of(k)

        def arrive(i, inner):
            source = j * per_sub + i

            @pl.when(source != me)
            def _():
                a2a_from(source).wait_recv()

            return inner

        lax.fori_loop(0, per_sub, arrive, 0)
        piece = rx[pl.ds(j * per_sub, per_sub)].reshape(2 * sub_rows, half + LANES)
        groups[0, j, :, :half] = jnp.dot(
            pick_low, piece[:, :half], preferred_element_type=jnp.float32
        ).astype(jnp.bfloat16)
        groups[0, j, :, half:width] = jnp.dot(
            pick_high, piece[:, :half], preferred_element_type=jnp.float32
        ).astype(jnp.bfloat16)
        groups[0, j, :, width:] = jnp.dot(
            pick_low, piece[:, half:], preferred_element_type=jnp.float32
        ).astype(jnp.bfloat16)
        y_first(j).start()
        sib_copy(0, j, 0, 1).start()
        return carry

    lax.fori_loop(0, subs, gather_sub, 0)

    def pass_on(k, carry):
        j = sub_of(k)
        y_first(j).wait_recv()
        y_second(j).start()
        return carry

    lax.fori_loop(0, subs, pass_on, 0)

    for k in range(split):
        to_right[k + split].wait_recv()
        to_left[k].wait_recv()
    widen(1)
    shift_block(1)
    widen(2)
    shift_block(2)
    for k in range(split):
        on_right[k].wait_recv()
        on_left[k + split].wait_recv()
    widen(3)
    shift_block(3)

    wide = n_x * LANES
    col = lax.broadcasted_iota(jnp.int32, (1, wide), 1)
    nth = lax.div(col, LANES)
    away = jnp.where(nth == 0, 0, jnp.where(nth == 1, n_x - 1, jnp.where(nth == 2, 1, 2)))
    block_at = block_of(yh, lax.rem(x + away, n_x), core)
    index = (block_at * LANES + lax.rem(col, LANES)).astype(jnp.float32)
    m = 2 * slots

    def score_pair(pair):
        bounds = groups[2 * pair:2 * pair + 2, :, :, width:].reshape(m, LANES).astype(jnp.float32)
        lane = lax.broadcasted_iota(jnp.int32, (m, LANES), 1)
        low = jnp.sum(
            jnp.where(lane == 0, bounds * 64.0, jnp.where(lane == 1, bounds, 0.0)), axis=1, keepdims=True
        )
        high = jnp.sum(
            jnp.where(lane == 2, bounds * 64.0, jnp.where(lane == 3, bounds, 0.0)), axis=1, keepdims=True
        )
        weight[...] = jnp.where((index >= low) & (index < high), 1.0, 0.0)
        res[2 * pair:2 * pair + 2] = jnp.zeros((2, slots, LANES), jnp.float32)

        def one(o, carry):
            spectra = groups[2 * pair:2 * pair + 2, :, :, :width].reshape(m, width)
            scores = jnp.dot(spectra, shifted[o], preferred_element_type=jnp.float32)
            level = jnp.maximum(scores, 0.0)
            kept = level * level * weight[...]
            summed = jnp.sum(kept, axis=1, keepdims=True)
            here = lax.broadcasted_iota(jnp.int32, (m, LANES), 1) == o
            old = res[2 * pair:2 * pair + 2].reshape(m, LANES)
            res[2 * pair:2 * pair + 2] = jnp.where(here, summed, old).reshape(2, slots, LANES)
            return carry

        lax.fori_loop(0, n_off, one, 0)

    def part_copy(g, device):
        return pltpu.make_async_remote_copy(
            src_ref=res.at[g], dst_ref=part.at[g - 1],
            send_sem=part_send.at[g - 1], recv_sem=part_recv.at[g - 1],
            device_id=device, device_id_type=MESH,
        )

    parts = [part_copy(1, sibling), part_copy(2, across), part_copy(3, diagonal)]

    def all_subs(body):
        def one(k, carry):
            body(sub_of(k))
            return carry

        lax.fori_loop(0, subs, one, 0)

    all_subs(lambda j: sib_copy(0, j, 0, 1).wait_recv())
    score_pair(0)
    parts[0].start()

    def relay(j):
        y_second(j).wait_recv()
        sib_copy(1, j, 2, 3).start()

    all_subs(relay)
    all_subs(lambda j: sib_copy(1, j, 2, 3).wait_recv())
    score_pair(1)
    parts[1].start()
    parts[2].start()
    for one_part in parts:
        one_part.wait_recv()
    total[...] = (res[0] + part[0] + part[1] + part[2]).reshape(n_range, cap, LANES)

    def back(k):
        there = lax.rem(me + k, n_range)
        return pltpu.make_async_remote_copy(
            src_ref=total.at[there], dst_ref=ret.at[me],
            send_sem=ret_send.at[there], recv_sem=ret_recv.at[me],
            device_id={"range": there}, device_id_type=MESH,
        )

    def back_from(source):
        return pltpu.make_async_remote_copy(
            src_ref=total.at[source], dst_ref=ret.at[source],
            send_sem=ret_send.at[source], recv_sem=ret_recv.at[source],
            device_id={"range": source}, device_id_type=MESH,
        )

    def start_back(k, carry):
        back(k).start()
        return carry

    lax.fori_loop(1, n_range, start_back, 0)
    ret[me] = total[me]

    def finish_sends(k, carry):
        a2a(k).wait_send()
        return carry

    lax.fori_loop(1, n_range, finish_sends, 0)
    for copies in (to_right, to_left, on_right, on_left):
        for k in copies:
            copies[k].wait_send()

    def finish_groups(j):
        y_first(j).wait_send()
        y_second(j).wait_send()
        sib_copy(0, j, 0, 1).wait_send()
        sib_copy(1, j, 2, 3).wait_send()

    all_subs(finish_groups)
    for one_part in parts:
        one_part.wait_send()

    def finish_back(k, carry):
        back_from(lax.rem(me + k, n_range)).wait_recv()
        return carry

    lax.fori_loop(1, n_range, finish_back, 0)

    t_wide = column_to_row(target, q_count, q_count)
    p = lax.broadcasted_iota(jnp.int32, (q_count, q_count), 0)
    c = lax.broadcasted_iota(jnp.int32, (q_count, q_count), 1)
    place = jnp.sum(jnp.where((target == t_wide) & (c < p), 1.0, 0.0), axis=1, keepdims=True)
    slot_column = target * cap + place
    spot = lax.broadcasted_iota(jnp.int32, (q_count, slots), 1).astype(jnp.float32)
    choose = jnp.where(spot == slot_column, 1.0, 0.0)
    answer = jnp.dot(
        choose, ret[...].reshape(slots, LANES),
        precision=lax.Precision.HIGHEST, preferred_element_type=jnp.float32,
    )
    span = (windows_ref[:, 1:2] - windows_ref[:, 0:1]).astype(jnp.float32) * float(width)
    out_ref[...] = (answer / span)[:, :n_off]

    def finish_returns(k, carry):
        back(k).wait_send()
        return carry

    lax.fori_loop(1, n_range, finish_returns, 0)


def local(queries, routing, windows, shifts, library):
    n_range = lax.axis_size("range")
    n_x = lax.axis_size("blk") // 4
    q_count, width = queries.shape
    lib_dev = library.shape[0]
    n_off = shifts.shape[0]
    cap = q_count // 4
    slots = n_range * cap
    subs = 4
    pieces = 4
    bf16, f32 = jnp.bfloat16, jnp.float32
    dma = pltpu.SemaphoreType.DMA
    vmem = pl.BlockSpec(memory_space=pltpu.VMEM)
    return pl.pallas_call(
        functools.partial(kernel, n_range, n_x, (q_count, width, cap, lib_dev, n_off)),
        out_shape=jax.ShapeDtypeStruct((q_count, n_off), f32),
        in_specs=[vmem, vmem, vmem, pl.BlockSpec(memory_space=pltpu.SMEM), vmem],
        out_specs=vmem,
        scratch_shapes=[
            pltpu.VMEM((n_range, 2 * cap, width // 2 + LANES), bf16),
            pltpu.VMEM((n_range, 2 * cap, width // 2 + LANES), bf16),
            pltpu.VMEM((4, subs, slots // subs, width + LANES), bf16),
            pltpu.VMEM((subs, slots // subs, width + LANES), bf16),
            pltpu.VMEM((n_x, pieces, width // pieces, lib_dev), bf16),
            pltpu.VMEM((n_x, width + 2 * PAD, lib_dev), f32),
            pltpu.VMEM((n_off, width, n_x * lib_dev), bf16),
            pltpu.VMEM((2 * slots, n_x * lib_dev), f32),
            pltpu.VMEM((4, slots, LANES), f32),
            pltpu.VMEM((3, slots, LANES), f32),
            pltpu.VMEM((n_range, cap, LANES), f32),
            pltpu.VMEM((n_range, cap, LANES), f32),
            dma((3, pieces)), dma((3, pieces)),
            dma((n_range,)), dma((n_range,)),
            dma((2, subs)), dma((2, subs)),
            dma((2, subs)), dma((2, subs)),
            dma((3,)), dma((3,)),
            dma((n_range,)), dma((n_range,)),
        ],
        compiler_params=pltpu.CompilerParams(
            collective_id=0, has_side_effects=True, vmem_limit_bytes=56 * 1024 * 1024
        ),
    )(queries, routing, windows, shifts, library)


def solution(mesh):
    both = ("range", "blk")
    in_specs = (P(both, None), P(both, None), P(both, None), P(), P(both, None))
    return jax.shard_map(
        local, mesh=mesh, in_specs=in_specs, out_specs=P(both, None), check_vma=False
    )
```

time: 134 us -> 67.1 us (0.50)
  Pallas kernels: 0 us -> 63.3 us
  waiting for transfers between devices: 35.4 us -> 0 us
  between operations: 28.3 us -> 0.01 us
  other arithmetic: 18.1 us -> 0 us
  starting transfers between devices: 17.7 us -> 0 us
  matrix products: 15.2 us -> 0 us
  blocking collectives: 15 us -> 0 us
    pallas_call x0 -> x1, Pallas kernels: none -> 63.3 us  [local(): pl.pallas_call(functools.partial(kernel, n_range, n_x, (q_count, width, c...]
    all_gather x1 -> x0, waiting for transfers between devices: 20.7 us -> none  [local(): lax.all_gather(library, 'blk', axis=0, tiled=True)]
    all_to_all x2 -> x0, starting transfers between devices: 17.7 us -> none  [the longest x1 10.1 us: local(): lax.all_to_all(bounds.reshape(n_range, per_range, 2), 'range', split_axis...]
    dot_general x3 -> x0, matrix products: 15.2 us -> none  [the longest x1 13.2 us: window_terms(): lax.dot_general(copies, block, (((2,), (1,)), ((), ())), preferred_elemen...]
    all_to_all x1 -> x0, blocking collectives: 15 us -> none  [local(): lax.all_to_all(results.reshape(n_range, per_range, n_offsets), 'range', s...]
    all_to_all x2 -> x0, waiting for transfers between devices: 14 us -> none  [the longest x1 14 us: local(): lax.all_to_all(outgoing.reshape(n_range, per_range, width), 'range', spli...]
    unnamed x7 -> x0, other arithmetic: 8.99 us -> none
    and x9 -> x0, other arithmetic: 5.4 us -> none  [the longest x8 4.93 us: shift_copies(): keep = (source >= 0) & (source < width)]
  transfers between devices with their start and end apart: 3 -> 0, of which waited for: 2 -> 0; matrix products, arithmetic and copies ran while one was open for 17% -> 0% of each run, Pallas kernels for 0% -> 0%
where the time goes in v1:
time: 67.1 us; the launch traced here: 66.7 us
  Pallas kernels  63.3 us (94%)
  local copies, waits for them, and re-layouts  3.41 us (5%)
    pallas_call x1, Pallas kernels, local(): pl.pallas_call(functools.partial(kernel, n_range, n_x, (q_count, width, c...  63.3 us
    unnamed x4, local copies, waits for them, and re-layouts  2.04 us
    pallas_call x1, local copies, waits for them, and re-layouts, local(): pl.pallas_call(functools.partial(kernel, n_range, n_x, (q_count, width, c...  1.38 us

profile of v1, /device:TPU:1, one launch (start us, length us, event | category | flops | bytes accessed | tf_op | source)
XLA Modules:
  0.0 66.7 jit_solution(4969622244447099218)
XLA Ops:
  0.0 0.0 copy-start
  0.0 1.3 %copy.6.routing_ref = s32[32,1]{1,0:T(8,128)} copy(s32[32,1]{0,1:T(1,128)} %param.6) | data formatting | bytes 256 | tf_op args[1]
  1.4 0.0 copy-done
  1.4 0.7 %copy.7.windows_ref = s32[32,2]{1,0:T(8,128)} copy(s32[32,2]{0,1:T(2,128)S(1)} %copy-done) | data formatting | bytes 512 | tf_op args[2]
  2.0 63.3 %shard_map.55 = f32[32,8]{1,0:T(8,128)} custom-call(bf16[32,2048]{1,0:T(8,128)(2,1)} %q_ref.1, s32[32,1]{1,0:T(8,128)} %copy.6.routing_ref, s32[32,2]{1,0:T(8,128)} %copy.7.windows_ref, s32[8]{0:T(128)} %shifts_ref.1, bf16[128,2048]{1,0:T(8,128)(2,1)} %lib_ref.1), custom_call_target="tpu_custom_call" | custom-call | tf_op jit(solution)/shard_map/pallas_call | solution.py:418
  65.3 1.4 %copy.8 = f32[32,8]{0,1:T(8,128)} copy(f32[32,8]{1,0:T(8,128)} %shard_map.55) | data formatting | bytes 2048 | tf_op jit(solution)/shard_map/pallas_call | solution.py:418
Async XLA Ops:
  0.0 1.4 %copy-start = (s32[32,2]{0,1:T(2,128)S(1)}, s32[32,2]{0,1:T(2,128)}, u32[]{:S(2)}) copy-start(s32[32,2]{0,1:T(2,128)} %param.7) | copy-start | bytes 772

commit v2 on v0

v2 whole, which is shorter than its diff:
```python
import functools

import jax
import jax.numpy as jnp
from jax import lax
from jax.experimental import pallas as pl
from jax.experimental.pallas import tpu as pltpu
from jax.sharding import PartitionSpec as P

MESH = pl.DeviceIdType.MESH
LANES = 128
PAD = 256
INVERSE = (0, 2, 1, 3)


def kernel(
    n_z, n_x, sizes,
    q_ref, routing_ref, windows_ref, shifts_ref, lib_ref, out_ref,
    tx, rx, groups, other, lt, padded, shifted, weight, acc, res, part_out, part, total, ret,
    z_send, z_recv, y_send, y_recv, sib_send, sib_recv, lib_send, lib_recv,
    part_send, part_recv, ret_send, ret_recv,
):
    q_count, width, cap, n_off = sizes
    n_pos = n_z // 2
    slots = 2 * n_z * cap
    pair = 2 * cap
    f32, bf16 = jnp.float32, jnp.bfloat16
    me = lax.axis_index("range")
    blk = lax.axis_index("blk")
    core = lax.rem(blk, 2)
    x = lax.rem(lax.div(blk, 2), n_x)
    yh = lax.div(blk, 2 * n_x)
    z = lax.div(me, 2)
    yl = lax.rem(me, 2)
    y = yh * 2 + yl

    def device(dz, dy, dx, dc):
        y_there = lax.rem(y + dy, 4)
        x_there = lax.rem(x + dx, n_x)
        return {
            "range": lax.rem(z + dz, n_z) * 2 + lax.rem(y_there, 2),
            "blk": lax.div(y_there, 2) * (2 * n_x) + x_there * 2 + lax.rem(core + dc, 2),
        }

    def remote(src, dst, send, recv, there):
        return pltpu.make_async_remote_copy(
            src_ref=src, dst_ref=dst, send_sem=send, recv_sem=recv,
            device_id=there, device_id_type=MESH,
        )

    y_step = (0, 1, 3, 2)
    barrier = pltpu.get_barrier_semaphore()
    greeted = [device(dz, 0, 0, 0) for dz in range(1, n_z)]
    greeted += [device(0, y_step[k], 0, dc) for k in range(4) for dc in range(2) if k or dc]
    greeted += [device(0, 0, dx, 0) for dx in range(1, n_x)]
    for there in greeted:
        pl.semaphore_signal(barrier, inc=1, device_id=there, device_id_type=MESH)

    t_row = routing_ref[...].astype(f32)
    p = lax.broadcasted_iota(jnp.int32, (q_count, q_count), 0)
    c = lax.broadcasted_iota(jnp.int32, (q_count, q_count), 1)
    t_column = jnp.sum(jnp.where(p == c, t_row, 0.0), axis=1, keepdims=True)
    earlier = (t_column == t_row) & (p < c)
    place = jnp.sum(jnp.where(earlier, 1.0, 0.0), axis=0, keepdims=True)
    slot_row = t_row * cap + place
    r = lax.broadcasted_iota(jnp.int32, (slots, q_count), 0).astype(f32)
    table = jnp.where(r == slot_row, 1.0, 0.0).astype(bf16)
    tx[:, :, :width] = (
        jnp.dot(table, q_ref[...], preferred_element_type=f32).astype(bf16).reshape(n_z, pair, width)
    )
    first = windows_ref[0:1, :]
    last = windows_ref[1:2, :]
    line = lax.broadcasted_iota(jnp.int32, (LANES, q_count), 0)
    coded = jnp.where(
        line == 0, lax.div(first, 64),
        jnp.where(line == 1, lax.rem(first, 64),
                  jnp.where(line == 2, lax.div(last, 64),
                            jnp.where(line == 3, lax.rem(last, 64), 0))))
    coded = coded.astype(f32).astype(bf16)
    tx[:, :, width:] = (
        lax.dot_general(table, coded, (((1,), (1,)), ((), ())), preferred_element_type=f32)
        .astype(bf16).reshape(n_z, pair, LANES)
    )
    rx[z] = tx[z]

    pieces = lt.shape[1]
    depth = width // pieces
    for k in range(pieces):
        block = lib_ref[:, k * depth:(k + 1) * depth].astype(f32).T
        padded[0, PAD + k * depth:PAD + (k + 1) * depth, :] = block
        lt[0, k] = block.astype(bf16)
    for b in range(n_x):
        padded[b, :PAD, :] = jnp.zeros((PAD, LANES), f32)
        padded[b, PAD + width:, :] = jnp.zeros((PAD, LANES), f32)

    pl.semaphore_wait(barrier, len(greeted))

    def z_copy(dz):
        there = lax.rem(z + dz, n_z)
        return remote(tx.at[there], rx.at[z], z_send.at[there], z_recv.at[z], device(dz, 0, 0, 0))

    def z_from(source):
        return remote(
            tx.at[source], rx.at[source], z_send.at[source], z_recv.at[source],
            device(lax.rem(source - z + n_z, n_z), 0, 0, 0),
        )

    def lib_copy(dx, k):
        landing = n_x - dx
        return remote(
            lt.at[0, k], lt.at[landing, k], lib_send.at[dx - 1, k], lib_recv.at[landing - 1, k],
            device(0, 0, dx, 0),
        )

    def lib_from(b, k):
        return remote(
            lt.at[0, k], lt.at[b, k], lib_send.at[b - 1, k], lib_recv.at[b - 1, k],
            device(0, 0, b, 0),
        )

    z_order = [1, n_z - 1, 2, n_z - 2, 3, n_z - 3, 4]
    for dz in z_order:
        z_copy(dz).start()
    for dx in (1, n_x - 1, 2):
        for k in range(pieces):
            lib_copy(dx, k).start()

    rows = 256

    def shift_block(b):
        def one(step, carry):
            o = lax.div(step, width // rows)
            at = pl.multiple_of(lax.rem(step, width // rows) * rows, rows)
            lane = pl.multiple_of(o * LANES, LANES)
            moved = padded[b, pl.ds(PAD + shifts_ref[o] + at, rows), :]
            shifted[b, pl.ds(at, rows), pl.ds(lane, LANES)] = moved.astype(bf16)
            return carry

        lax.fori_loop(0, n_off * (width // rows), one, 0)

    def take_block(b):
        for k in range(pieces):
            lib_from(b, k).wait_recv()
            padded[b, PAD + k * depth:PAD + (k + 1) * depth, :] = lt[b, k].astype(f32)
        shift_block(b)

    pr = lax.broadcasted_iota(jnp.int32, (2 * pair, 2 * pair), 0)
    pc = lax.broadcasted_iota(jnp.int32, (2 * pair, 2 * pair), 1)
    upper = lax.div(pr, pair)
    source_half = jnp.where(upper == 0, yl, 1 - yl)
    within = lax.rem(pr, pair)
    from_row = lax.div(within, cap) * pair + source_half * cap + lax.rem(within, cap)
    pick = jnp.where(pc == from_row, 1.0, 0.0).astype(bf16)
    home = lax.div(z, 2)
    hop = (0, n_pos - 1, 1, 2)

    def y_copy(k, pos):
        src = groups.at[pos, 0, 0] if k == 3 else other.at[pos]
        landing = INVERSE[k]
        return remote(
            src, groups.at[pos, 0, landing], y_send.at[k - 1, pos], y_recv.at[landing - 1, pos],
            device(0, y_step[k], 0, 0),
        )

    def y_from(k, pos):
        return remote(
            other.at[pos], groups.at[pos, 0, k], y_send.at[k - 1, pos], y_recv.at[k - 1, pos],
            device(0, y_step[k], 0, 0),
        )

    def sib_copy(k, pos):
        return remote(
            groups.at[pos, 0, k], groups.at[pos, 1, k], sib_send.at[k, pos], sib_recv.at[k, pos],
            device(0, 0, 0, 1),
        )

    def send_pos(pos):
        u = lax.rem(home + hop[pos], n_pos)
        for i in range(2):
            source = u * 2 + i

            @pl.when(source != z)
            def _():
                z_from(source).wait_recv()

        piece = rx[pl.ds(u * 2, 2)].reshape(2 * pair, width + LANES)
        parted = jnp.dot(pick, piece, preferred_element_type=f32).astype(bf16)
        groups[pos, 0, 0] = parted[:pair]
        other[pos] = parted[pair:]
        for k in (3, 1, 2):
            y_copy(k, pos).start()
        sib_copy(0, pos).start()

    def relay(pos):
        for k in (1, 2, 3):
            y_from(k, pos).wait_recv()
            sib_copy(k, pos).start()

    def settle(pos):
        for k in range(4):
            sib_copy(k, pos).wait_recv()

    wide = n_x * LANES
    col = lax.broadcasted_iota(jnp.int32, (1, wide), 1)
    block_at = yh * (2 * n_x) + lax.rem(x + lax.div(col, LANES), n_x) * 2 + core
    index = (block_at * LANES + lax.rem(col, LANES)).astype(f32)
    m = 8 * pair * 2

    def weigh(h):
        bounds = groups[2 * h:2 * h + 2, :, :, :, width:].reshape(m, LANES).astype(f32)
        lane = lax.broadcasted_iota(jnp.int32, (m, LANES), 1)
        low = jnp.sum(
            jnp.where(lane == 0, bounds * 64.0, jnp.where(lane == 1, bounds, 0.0)), axis=1, keepdims=True
        )
        high = jnp.sum(
            jnp.where(lane == 2, bounds * 64.0, jnp.where(lane == 3, bounds, 0.0)), axis=1, keepdims=True
        )
        weight[h] = jnp.where((index >= low) & (index < high), 1.0, 0.0)

    def score(h, b, fresh):
        spectra = groups[2 * h:2 * h + 2, :, :, :, :width].reshape(m, width)
        for part_of in range(2):
            at = part_of * 4 * LANES
            scores = jnp.dot(spectra, shifted[b, :, at:at + 4 * LANES], preferred_element_type=f32)
            for i in range(4):
                level = jnp.maximum(scores[:, i * LANES:(i + 1) * LANES], 0.0)
                kept = level * level * weight[h, :, b * LANES:(b + 1) * LANES]
                o = part_of * 4 + i
                acc[h, o] = kept if fresh else acc[h, o] + kept

    def gather_scores(h):
        lane = lax.broadcasted_iota(jnp.int32, (m, LANES), 1)
        value = jnp.zeros((m, LANES), f32)
        for o in range(n_off):
            value = jnp.where(lane == o, jnp.sum(acc[h, o], axis=1, keepdims=True), value)
        res[2 * h:2 * h + 2] = value.reshape(2, 2, 4, pair, LANES)

    shift_block(0)
    for pos in range(n_pos):
        send_pos(pos)
        if pos:
            relay(pos - 1)
    relay(n_pos - 1)
    for pos in range(n_pos):
        settle(pos)
    weigh(0)
    weigh(1)
    score(0, 0, True)
    score(1, 0, True)
    for b in (1, 3, 2):
        take_block(b)
        score(0, b, False)
        score(1, b, False)
    gather_scores(0)
    gather_scores(1)

    def part_copy(k, dc):
        return remote(
            part_out.at[2 * k + dc], part.at[2 * INVERSE[k] + dc],
            part_send.at[2 * k + dc], part_recv.at[2 * INVERSE[k] + dc],
            device(0, y_step[k], 0, dc),
        )

    def part_from(k, dc):
        return remote(
            part_out.at[2 * k + dc], part.at[2 * k + dc],
            part_send.at[2 * k + dc], part_recv.at[2 * k + dc],
            device(0, y_step[k], 0, dc),
        )

    lane = lax.broadcasted_iota(jnp.int32, (n_off, LANES), 1)
    mine = lax.div(lane, LANES // 2) == yl
    partners = [(k, dc) for k in (3, 1, 2, 0) for dc in range(2) if k or dc]
    for k, dc in partners + [(0, 0)]:
        column = res[:, dc, k].reshape(n_pos * pair, LANES)
        tile = jnp.concatenate([column, column], axis=0).T[:n_off]
        part_out[2 * k + dc] = jnp.where(mine, tile, 0.0)
        if k or dc:
            part_copy(k, dc).start()
    summed = part_out[0]
    for k, dc in partners:
        part_from(k, dc).wait_recv()
        summed = summed + part[2 * k + dc]
    total[...] = summed

    def ret_copy(dz):
        there = lax.rem(z + dz, n_z)
        return remote(total, ret.at[z], ret_send.at[there], ret_recv.at[z], device(dz, 0, 0, 0))

    def ret_from(dz):
        source = lax.rem(z + dz, n_z)
        return remote(
            total, ret.at[source], ret_send.at[source], ret_recv.at[source], device(dz, 0, 0, 0)
        )

    for dz in [4] + z_order[:-1][::-1]:
        ret_copy(dz).start()
    ret[z] = summed

    for dz in z_order:
        z_copy(dz).wait_send()
    for dx in range(1, n_x):
        for k in range(pieces):
            lib_copy(dx, k).wait_send()
    for pos in range(n_pos):
        for k in (1, 2, 3):
            y_copy(k, pos).wait_send()
        for k in range(4):
            sib_copy(k, pos).wait_send()
    for k, dc in partners:
        part_copy(k, dc).wait_send()

    half_row = jnp.floor(t_row * 0.5)
    z_there = half_row
    yl_there = t_row - 2.0 * half_row
    delta = home.astype(f32) - jnp.floor(z_there * 0.5)
    delta = jnp.where(delta < 0.0, delta + n_pos, delta)
    pos_there = jnp.where(delta == 0.0, 0.0, jnp.where(delta == n_pos - 1.0, 1.0, delta + 1.0))
    spot = (
        z_there * LANES + yl_there * (LANES // 2) + pos_there * pair
        + lax.rem(z, 2).astype(f32) * cap + place
    )
    line = lax.broadcasted_iota(jnp.int32, (n_z * LANES, q_count), 0).astype(f32)
    choose = jnp.where(line == spot, 1.0, 0.0)

    for dz in z_order:
        ret_from(dz).wait_recv()
    every = jnp.concatenate([ret[i] for i in range(n_z)], axis=1)
    answer = jnp.dot(every, choose, precision=lax.Precision.HIGHEST, preferred_element_type=f32)
    span = (last - first).astype(f32) * float(width)
    out_ref[...] = answer / span

    for dz in z_order:
        ret_copy(dz).wait_send()


def local(queries, routing, windows, shifts, library):
    n_z = lax.axis_size("range") // 2
    n_x = lax.axis_size("blk") // 4
    q_count, width = queries.shape
    lib_dev = library.shape[0]
    n_off = shifts.shape[0]
    cap = q_count // 4
    pair = 2 * cap
    n_pos = n_z // 2
    pieces = 2
    spectrum = width + LANES
    bf16, f32 = jnp.bfloat16, jnp.float32
    dma = pltpu.SemaphoreType.DMA
    vmem = pl.BlockSpec(memory_space=pltpu.VMEM)
    out = pl.pallas_call(
        functools.partial(kernel, n_z, n_x, (q_count, width, cap, n_off)),
        out_shape=jax.ShapeDtypeStruct((n_off, q_count), f32),
        in_specs=[vmem, vmem, vmem, pl.BlockSpec(memory_space=pltpu.SMEM), vmem],
        out_specs=vmem,
        scratch_shapes=[
            pltpu.VMEM((n_z, pair, spectrum), bf16),
            pltpu.VMEM((n_z, pair, spectrum), bf16),
            pltpu.VMEM((n_pos, 2, 4, pair, spectrum), bf16),
            pltpu.VMEM((n_pos, pair, spectrum), bf16),
            pltpu.VMEM((n_x, pieces, width // pieces, lib_dev), bf16),
            pltpu.VMEM((n_x, width + 2 * PAD, lib_dev), f32),
            pltpu.VMEM((n_x, width, n_off * lib_dev), bf16),
            pltpu.VMEM((2, 16 * pair, n_x * lib_dev), f32),
            pltpu.VMEM((2, n_off, 16 * pair, lib_dev), f32),
            pltpu.VMEM((n_pos, 2, 4, pair, LANES), f32),
            pltpu.VMEM((8, n_off, LANES), f32),
            pltpu.VMEM((8, n_off, LANES), f32),
            pltpu.VMEM((n_off, LANES), f32),
            pltpu.VMEM((n_z, n_off, LANES), f32),
            dma((n_z,)), dma((n_z,)),
            dma((3, n_pos)), dma((3, n_pos)),
            dma((4, n_pos)), dma((4, n_pos)),
            dma((n_x - 1, pieces)), dma((n_x - 1, pieces)),
            dma((8,)), dma((8,)),
            dma((n_z,)), dma((n_z,)),
        ],
        compiler_params=pltpu.CompilerParams(
            collective_id=0, has_side_effects=True, vmem_limit_bytes=56 * 1024 * 1024
        ),
    )(queries, routing.T, windows.T, shifts, library)
    return out.T


def solution(mesh):
    both = ("range", "blk")
    in_specs = (P(both, None), P(both, None), P(both, None), P(), P(both, None))
    return jax.shard_map(
        local, mesh=mesh, in_specs=in_specs, out_specs=P(both, None), check_vma=False
    )
```

time: 134 us -> 57.9 us (0.43)
  Pallas kernels: 0 us -> 56.3 us
  waiting for transfers between devices: 35.4 us -> 0 us
  between operations: 28.3 us -> 0.01 us
  other arithmetic: 18.1 us -> 0 us
  starting transfers between devices: 17.7 us -> 0 us
  matrix products: 15.2 us -> 0 us
  blocking collectives: 15 us -> 0 us
  local copies, waits for them, and re-layouts: 3.45 us -> 1.28 us
    pallas_call x0 -> x1, Pallas kernels: none -> 56.3 us  [local(): pl.pallas_call(functools.partial(kernel, n_z, n_x, (q_count, width, cap,...]
    all_gather x1 -> x0, waiting for transfers between devices: 20.7 us -> none  [local(): lax.all_gather(library, 'blk', axis=0, tiled=True)]
    all_to_all x2 -> x0, starting transfers between devices: 17.7 us -> none  [the longest x1 10.1 us: local(): lax.all_to_all(bounds.reshape(n_range, per_range, 2), 'range', split_axis...]
    dot_general x3 -> x0, matrix products: 15.2 us -> none  [the longest x1 13.2 us: window_terms(): lax.dot_general(copies, block, (((2,), (1,)), ((), ())), preferred_elemen...]
    all_to_all x1 -> x0, blocking collectives: 15 us -> none  [local(): lax.all_to_all(results.reshape(n_range, per_range, n_offsets), 'range', s...]
    all_to_all x2 -> x0, waiting for transfers between devices: 14 us -> none  [the longest x1 14 us: local(): lax.all_to_all(outgoing.reshape(n_range, per_range, width), 'range', spli...]
    unnamed x7 -> x0, other arithmetic: 8.99 us -> none
    and x9 -> x0, other arithmetic: 5.4 us -> none  [the longest x8 4.93 us: shift_copies(): keep = (source >= 0) & (source < width)]
  transfers between devices with their start and end apart: 3 -> 0, of which waited for: 2 -> 0; matrix products, arithmetic and copies ran while one was open for 17% -> 0% of each run, Pallas kernels for 0% -> 0%
where the time goes in v2:
time: 57.9 us; the launch traced here: 57.6 us
  Pallas kernels  56.3 us (97%)
  local copies, waits for them, and re-layouts  1.28 us (2%)
    pallas_call x1, Pallas kernels, local(): pl.pallas_call(functools.partial(kernel, n_z, n_x, (q_count, width, cap,...  56.3 us
    unnamed x1, local copies, waits for them, and re-layouts  1.28 us

profile of v2, /device:TPU:1, one launch (start us, length us, event | category | flops | bytes accessed | tf_op | source)
XLA Modules:
  0.0 57.6 jit_solution(14716926918122977373)
XLA Ops:
  0.0 56.3 %shard_map.55 = f32[8,32]{1,0:T(8,128)} custom-call(bf16[32,2048]{1,0:T(8,128)(2,1)} %q_ref.1, s32[1,32]{1,0:T(1,128)} %bitcast.5, s32[2,32]{1,0:T(2,128)} %bitcast.4, s32[8]{0:T(128)} %shifts_ref.1, bf16[128,2048]{1,0:T(8,128)(2,1)} %lib_ref.1), custom_call_target="tpu_custom_call" | custom-call | tf_op jit(solution)/shard_map/pallas_call | solution.py:351
  56.3 1.3 %copy.7 = f32[32,8]{0,1:T(8,128)} copy(f32[32,8]{0,1:T(8,128)} %bitcast.3) | data formatting | bytes 2048

commit v3 on v2

--- a/solution.py
+++ b/solution.py
@@ -52,7 +52,7 @@
     barrier = pltpu.get_barrier_semaphore()
     greeted = [device(dz, 0, 0, 0) for dz in range(1, n_z)]
     greeted += [device(0, y_step[k], 0, dc) for k in range(4) for dc in range(2) if k or dc]
-    greeted += [device(0, 0, dx, 0) for dx in range(1, n_x)]
+    greeted += [device(0, 0, dx, 0) for dx in (1, n_x - 1)]
     for there in greeted:
         pl.semaphore_signal(barrier, inc=1, device_id=there, device_id_type=MESH)
 
@@ -83,47 +83,61 @@
     )
     rx[z] = tx[z]
 
+    for b in range(n_x):
+        padded[b, :PAD, :] = jnp.zeros((PAD, LANES), f32)
+        padded[b, PAD + width:, :] = jnp.zeros((PAD, LANES), f32)
+    for pos in range(n_pos):
+        acc[pos] = jnp.zeros(acc.shape[1:], f32)
+
+    pl.semaphore_wait(barrier, len(greeted))
+
+    def z_copy(dz):
+        there = lax.rem(z + dz, n_z)
+        return remote(tx.at[there], rx.at[z], z_send.at[there], z_recv.at[z], device(dz, 0, 0, 0))
+
+    def z_from(source):
+        return remote(
+            tx.at[source], rx.at[source], z_send.at[source], z_recv.at[source],
+            device(lax.rem(source - z + n_z, n_z), 0, 0, 0),
+        )
+
+    def lib_copy(way, k):
+        source, landing, dx = ((0, 2, 1), (0, 1, n_x - 1), (2, 3, 1), (1, 3, n_x - 1))[way]
+        slot = min(way, 2)
+        return remote(
+            lt.at[source, k], lt.at[landing, k], lib_send.at[slot, k], lib_recv.at[slot, k],
+            device(0, 0, dx, 0),
+        )
+
+    z_order = [1, n_z - 1, 2, n_z - 2, 3, n_z - 3, 4]
+    for dz in z_order:
+        z_copy(dz).start()
     pieces = lt.shape[1]
     depth = width // pieces
+    split = pieces // 2
     for k in range(pieces):
         block = lib_ref[:, k * depth:(k + 1) * depth].astype(f32).T
         padded[0, PAD + k * depth:PAD + (k + 1) * depth, :] = block
         lt[0, k] = block.astype(bf16)
-    for b in range(n_x):
-        padded[b, :PAD, :] = jnp.zeros((PAD, LANES), f32)
-        padded[b, PAD + width:, :] = jnp.zeros((PAD, LANES), f32)
-
-    pl.semaphore_wait(barrier, len(greeted))
-
-    def z_copy(dz):
-        there = lax.rem(z + dz, n_z)
-        return remote(tx.at[there], rx.at[z], z_send.at[there], z_recv.at[z], device(dz, 0, 0, 0))
-
-    def z_from(source):
-        return remote(
-            tx.at[source], rx.at[source], z_send.at[source], z_recv.at[source],
-            device(lax.rem(source - z + n_z, n_z), 0, 0, 0),
-        )
-
-    def lib_copy(dx, k):
-        landing = n_x - dx
-        return remote(
-            lt.at[0, k], lt.at[landing, k], lib_send.at[dx - 1, k], lib_recv.at[landing - 1, k],
-            device(0, 0, dx, 0),
-        )
-
-    def lib_from(b, k):
-        return remote(
-            lt.at[0, k], lt.at[b, k], lib_send.at[b - 1, k], lib_recv.at[b - 1, k],
-            device(0, 0, b, 0),
-        )
-
-    z_order = [1, n_z - 1, 2, n_z - 2, 3, n_z - 3, 4]
-    for dz in z_order:
-        z_copy(dz).start()
-    for dx in (1, n_x - 1, 2):
-        for k in range(pieces):
-            lib_copy(dx, k).start()
+        if k % split == split - 1:
+            for i in range(k - split + 1, k + 1):
+                lib_copy(k // split, i).start()
+    for i in range(split):
+        lib_copy(0, split + i).start()
+        lib_copy(1, i).start()
+
+    def forward(i):
+        lib_copy(0, i).wait_recv()
+        lib_copy(2, i).start()
+        lib_copy(1, split + i).wait_recv()
+        lib_copy(3, split + i).start()
+
+    def lib_ways(b):
+        if b == 3:
+            return [(2, i) for i in range(split)] + [(3, split + i) for i in range(split)]
+        if b == 2:
+            return [(0, split + i) for i in range(split)]
+        return [(1, i) for i in range(split)]
 
     rows = 256
 
@@ -139,8 +153,9 @@
         lax.fori_loop(0, n_off * (width // rows), one, 0)
 
     def take_block(b):
+        for way, k in lib_ways(b):
+            lib_copy(way, k).wait_recv()
         for k in range(pieces):
-            lib_from(b, k).wait_recv()
             padded[b, PAD + k * depth:PAD + (k + 1) * depth, :] = lt[b, k].astype(f32)
         shift_block(b)
 
@@ -152,7 +167,8 @@
     from_row = lax.div(within, cap) * pair + source_half * cap + lax.rem(within, cap)
     pick = jnp.where(pc == from_row, 1.0, 0.0).astype(bf16)
     home = lax.div(z, 2)
-    hop = (0, n_pos - 1, 1, 2)
+    odd = lax.rem(z, 2)
+    hop = (0, n_pos - 1 - odd * (n_pos - 2), 1 + odd * (n_pos - 2), 2)
 
     def y_copy(k, pos):
         src = groups.at[pos, 0, 0] if k == 3 else other.at[pos]
@@ -202,12 +218,14 @@
 
     wide = n_x * LANES
     col = lax.broadcasted_iota(jnp.int32, (1, wide), 1)
-    block_at = yh * (2 * n_x) + lax.rem(x + lax.div(col, LANES), n_x) * 2 + core
+    nth = lax.div(col, LANES)
+    away = jnp.where(nth == 2, n_x - 1, jnp.where(nth == 3, 2, nth))
+    block_at = yh * (2 * n_x) + lax.rem(x + away, n_x) * 2 + core
     index = (block_at * LANES + lax.rem(col, LANES)).astype(f32)
-    m = 8 * pair * 2
-
-    def weigh(h):
-        bounds = groups[2 * h:2 * h + 2, :, :, :, width:].reshape(m, LANES).astype(f32)
+    m = 8 * pair
+
+    def weigh(pos):
+        bounds = groups[pos, :, :, :, width:].reshape(m, LANES).astype(f32)
         lane = lax.broadcasted_iota(jnp.int32, (m, LANES), 1)
         low = jnp.sum(
             jnp.where(lane == 0, bounds * 64.0, jnp.where(lane == 1, bounds, 0.0)), axis=1, keepdims=True
@@ -215,44 +233,57 @@
         high = jnp.sum(
             jnp.where(lane == 2, bounds * 64.0, jnp.where(lane == 3, bounds, 0.0)), axis=1, keepdims=True
         )
-        weight[h] = jnp.where((index >= low) & (index < high), 1.0, 0.0)
-
-    def score(h, b, fresh):
-        spectra = groups[2 * h:2 * h + 2, :, :, :, :width].reshape(m, width)
-        for part_of in range(2):
-            at = part_of * 4 * LANES
-            scores = jnp.dot(spectra, shifted[b, :, at:at + 4 * LANES], preferred_element_type=f32)
-            for i in range(4):
-                level = jnp.maximum(scores[:, i * LANES:(i + 1) * LANES], 0.0)
-                kept = level * level * weight[h, :, b * LANES:(b + 1) * LANES]
-                o = part_of * 4 + i
-                acc[h, o] = kept if fresh else acc[h, o] + kept
-
-    def gather_scores(h):
+        inside = jnp.where((index >= low) & (index < high), 1.0, 0.0)
+        for b in range(n_x):
+            weight[pos, b] = inside[:, b * LANES:(b + 1) * LANES]
+
+    def score(pos, count, *blocks):
+        spectra = groups[pos:pos + count, :, :, :, :width].reshape(count * m, width)
+        for b in blocks:
+            for half in range(2):
+                at = half * 4 * LANES
+                scores = jnp.dot(spectra, shifted[b, :, at:at + 4 * LANES], preferred_element_type=f32)
+                for i in range(4):
+                    level = jnp.maximum(scores[:, i * LANES:(i + 1) * LANES], 0.0)
+                    kept = (level * level).reshape(count, m, LANES) * weight[pos:pos + count, b]
+                    acc[pos:pos + count, half * 4 + i] += kept
+
+    def gather_scores(pos):
         lane = lax.broadcasted_iota(jnp.int32, (m, LANES), 1)
         value = jnp.zeros((m, LANES), f32)
         for o in range(n_off):
-            value = jnp.where(lane == o, jnp.sum(acc[h, o], axis=1, keepdims=True), value)
-        res[2 * h:2 * h + 2] = value.reshape(2, 2, 4, pair, LANES)
+            value = jnp.where(lane == o, jnp.sum(acc[pos, o], axis=1, keepdims=True), value)
+        res[pos] = value.reshape(2, 4, pair, LANES)
 
     shift_block(0)
-    for pos in range(n_pos):
-        send_pos(pos)
-        if pos:
-            relay(pos - 1)
-    relay(n_pos - 1)
-    for pos in range(n_pos):
-        settle(pos)
+    send_pos(0)
+    forward(0)
+    send_pos(1)
+    forward(1)
+    relay(0)
+    send_pos(2)
+    relay(1)
+    send_pos(3)
+    settle(0)
+    settle(1)
     weigh(0)
     weigh(1)
-    score(0, 0, True)
-    score(1, 0, True)
-    for b in (1, 3, 2):
-        take_block(b)
-        score(0, b, False)
-        score(1, b, False)
-    gather_scores(0)
-    gather_scores(1)
+    take_block(1)
+    take_block(2)
+    relay(2)
+    score(0, 2, 0, 1)
+    relay(3)
+    settle(2)
+    weigh(2)
+    score(0, 3, 2)
+    score(2, 1, 0, 1)
+    take_block(3)
+    settle(3)
+    weigh(3)
+    score(0, 4, 3)
+    score(3, 1, 0, 1, 2)
+    for pos in range(n_pos):
+        gather_scores(pos)
 
     def part_copy(k, dc):
         return remote(
@@ -299,9 +330,8 @@
 
     for dz in z_order:
         z_copy(dz).wait_send()
-    for dx in range(1, n_x):
-        for k in range(pieces):
-            lib_copy(dx, k).wait_send()
+    for way, k in [(w, k) for w in range(2) for k in range(pieces)] + lib_ways(3):
+        lib_copy(way, k).wait_send()
     for pos in range(n_pos):
         for k in (1, 2, 3):
             y_copy(k, pos).wait_send()
@@ -315,7 +345,9 @@
     yl_there = t_row - 2.0 * half_row
     delta = home.astype(f32) - jnp.floor(z_there * 0.5)
     delta = jnp.where(delta < 0.0, delta + n_pos, delta)
-    pos_there = jnp.where(delta == 0.0, 0.0, jnp.where(delta == n_pos - 1.0, 1.0, delta + 1.0))
+    z_odd = z_there - 2.0 * jnp.floor(z_there * 0.5)
+    second = jnp.where(z_odd == 0.0, n_pos - 1.0, 1.0)
+    pos_there = jnp.where(delta == 0.0, 0.0, jnp.where(delta == second, 1.0, jnp.where(delta == 2.0, 3.0, 2.0)))
     spot = (
         z_there * LANES + yl_there * (LANES // 2) + pos_there * pair
         + lax.rem(z, 2).astype(f32) * cap + place
@@ -343,7 +375,7 @@
     cap = q_count // 4
     pair = 2 * cap
     n_pos = n_z // 2
-    pieces = 2
+    pieces = 4
     spectrum = width + LANES
     bf16, f32 = jnp.bfloat16, jnp.float32
     dma = pltpu.SemaphoreType.DMA
@@ -361,8 +393,8 @@
             pltpu.VMEM((n_x, pieces, width // pieces, lib_dev), bf16),
             pltpu.VMEM((n_x, width + 2 * PAD, lib_dev), f32),
             pltpu.VMEM((n_x, width, n_off * lib_dev), bf16),
-            pltpu.VMEM((2, 16 * pair, n_x * lib_dev), f32),
-            pltpu.VMEM((2, n_off, 16 * pair, lib_dev), f32),
+            pltpu.VMEM((n_pos, n_x, 8 * pair, lib_dev), f32),
+            pltpu.VMEM((n_pos, n_off, 8 * pair, lib_dev), f32),
             pltpu.VMEM((n_pos, 2, 4, pair, LANES), f32),
             pltpu.VMEM((8, n_off, LANES), f32),
             pltpu.VMEM((8, n_off, LANES), f32),
@@ -371,7 +403,7 @@
             dma((n_z,)), dma((n_z,)),
             dma((3, n_pos)), dma((3, n_pos)),
             dma((4, n_pos)), dma((4, n_pos)),
-            dma((n_x - 1, pieces)), dma((n_x - 1, pieces)),
+            dma((3, pieces)), dma((3, pieces)),
             dma((8,)), dma((8,)),
             dma((n_z,)), dma((n_z,)),
         ],

time: 57.9 us -> 51.5 us (0.89)
  Pallas kernels: 56.3 us -> 49.9 us
    pallas_call x1, Pallas kernels: 56.3 us -> 49.9 us  [local(): pl.pallas_call(functools.partial(kernel, n_z, n_x, (q_count, width, cap,...]
where the time goes in v3:
time: 51.5 us; the launch traced here: 51.2 us
  Pallas kernels  49.9 us (97%)
  local copies, waits for them, and re-layouts  1.28 us (2%)
    pallas_call x1, Pallas kernels, local(): pl.pallas_call(functools.partial(kernel, n_z, n_x, (q_count, width, cap,...  49.9 us
    unnamed x1, local copies, waits for them, and re-layouts  1.28 us

profile of v3, /device:TPU:1, one launch (start us, length us, event | category | flops | bytes accessed | tf_op | source)
XLA Modules:
  0.0 51.2 jit_solution(6395692326336917283)
XLA Ops:
  0.0 49.9 %shard_map.55 = f32[8,32]{1,0:T(8,128)} custom-call(bf16[32,2048]{1,0:T(8,128)(2,1)} %q_ref.1, s32[1,32]{1,0:T(1,128)} %bitcast.5, s32[2,32]{1,0:T(2,128)} %bitcast.4, s32[8]{0:T(128)} %shifts_ref.1, bf16[128,2048]{1,0:T(8,128)(2,1)} %lib_ref.1), custom_call_target="tpu_custom_call" | custom-call | tf_op jit(solution)/shard_map/pallas_call | solution.py:383
  49.9 1.3 %copy.7 = f32[32,8]{0,1:T(8,128)} copy(f32[32,8]{0,1:T(8,128)} %bitcast.3) | data formatting | bytes 2048

commit v4 on v3

--- a/solution.py
+++ b/solution.py
@@ -260,23 +260,26 @@
     forward(0)
     send_pos(1)
     forward(1)
+    send_pos(2)
     relay(0)
-    send_pos(2)
+    take_block(1)
     relay(1)
+    settle(0)
+    weigh(0)
+    score(0, 1, 0)
     send_pos(3)
-    settle(0)
     settle(1)
-    weigh(0)
     weigh(1)
-    take_block(1)
+    score(0, 1, 1)
+    score(1, 1, 0, 1)
+    relay(2)
     take_block(2)
-    relay(2)
-    score(0, 2, 0, 1)
-    relay(3)
+    score(0, 2, 2)
     settle(2)
     weigh(2)
-    score(0, 3, 2)
-    score(2, 1, 0, 1)
+    score(2, 1, 0)
+    relay(3)
+    score(2, 1, 1, 2)
     take_block(3)
     settle(3)
     weigh(3)

time: 51.5 us -> 49.9 us (0.969)
  Pallas kernels: 49.9 us -> 48.5 us
    pallas_call x1, Pallas kernels: 49.9 us -> 48.5 us  [local(): pl.pallas_call(functools.partial(kernel, n_z, n_x, (q_count, width, cap,...]
where the time goes in v4:
time: 49.9 us; the launch traced here: 49.8 us
  Pallas kernels  48.5 us (97%)
  local copies, waits for them, and re-layouts  1.28 us (3%)
    pallas_call x1, Pallas kernels, local(): pl.pallas_call(functools.partial(kernel, n_z, n_x, (q_count, width, cap,...  48.5 us
    unnamed x1, local copies, waits for them, and re-layouts  1.28 us

profile of v4, /device:TPU:1, one launch (start us, length us, event | category | flops | bytes accessed | tf_op | source)
XLA Modules:
  0.0 49.8 jit_solution(8818239071259678383)
XLA Ops:
  0.0 48.5 %shard_map.55 = f32[8,32]{1,0:T(8,128)} custom-call(bf16[32,2048]{1,0:T(8,128)(2,1)} %q_ref.1, s32[1,32]{1,0:T(1,128)} %bitcast.5, s32[2,32]{1,0:T(2,128)} %bitcast.4, s32[8]{0:T(128)} %shifts_ref.1, bf16[128,2048]{1,0:T(8,128)(2,1)} %lib_ref.1), custom_call_target="tpu_custom_call" | custom-call | tf_op jit(solution)/shard_map/pallas_call | solution.py:386
  48.5 1.3 %copy.7 = f32[32,8]{0,1:T(8,128)} copy(f32[32,8]{0,1:T(8,128)} %bitcast.3) | data formatting | bytes 2048

commit v5 on v4

--- a/solution.py
+++ b/solution.py
@@ -110,8 +110,9 @@
         )
 
     z_order = [1, n_z - 1, 2, n_z - 2, 3, n_z - 3, 4]
-    for dz in z_order:
-        z_copy(dz).start()
+    turn = 1 - 2 * lax.rem(z, 2)
+    for d in (1, -1, 2, -2, 3, -3, 4):
+        z_copy(lax.rem(n_z + d * turn, n_z)).start()
     pieces = lt.shape[1]
     depth = width // pieces
     split = pieces // 2
@@ -277,16 +278,16 @@
     score(0, 2, 2)
     settle(2)
     weigh(2)
-    score(2, 1, 0)
+    score(2, 1, 0, 1, 2)
+    take_block(3)
     relay(3)
-    score(2, 1, 1, 2)
-    take_block(3)
+    score(0, 3, 3)
+    for pos in range(n_pos - 1):
+        gather_scores(pos)
     settle(3)
     weigh(3)
-    score(0, 4, 3)
-    score(3, 1, 0, 1, 2)
-    for pos in range(n_pos):
-        gather_scores(pos)
+    score(3, 1, 0, 1, 2, 3)
+    gather_scores(n_pos - 1)
 
     def part_copy(k, dc):
         return remote(
@@ -356,12 +357,16 @@
         + lax.rem(z, 2).astype(f32) * cap + place
     )
     line = lax.broadcasted_iota(jnp.int32, (n_z * LANES, q_count), 0).astype(f32)
-    choose = jnp.where(line == spot, 1.0, 0.0)
+    choose = jnp.where(line == spot, 1.0, 0.0).astype(bf16)
 
     for dz in z_order:
         ret_from(dz).wait_recv()
     every = jnp.concatenate([ret[i] for i in range(n_z)], axis=1)
-    answer = jnp.dot(every, choose, precision=lax.Precision.HIGHEST, preferred_element_type=f32)
+    high = every.astype(bf16).astype(f32)
+    middle = (every - high).astype(bf16).astype(f32)
+    thirds = jnp.concatenate([high, middle, every - high - middle], axis=0).astype(bf16)
+    picked = jnp.dot(thirds, choose, preferred_element_type=f32)
+    answer = picked[2 * n_off:] + picked[n_off:2 * n_off] + picked[:n_off]
     span = (last - first).astype(f32) * float(width)
     out_ref[...] = answer / span
 

time: 49.9 us -> 49.8 us (level)
  no operation moved by 1% of the time
where the time goes in v5:
time: 49.8 us; the launch traced here: 49.7 us
  Pallas kernels  48.4 us (97%)
  local copies, waits for them, and re-layouts  1.28 us (3%)
    pallas_call x1, Pallas kernels, local(): pl.pallas_call(functools.partial(kernel, n_z, n_x, (q_count, width, cap,...  48.4 us
    unnamed x1, local copies, waits for them, and re-layouts  1.28 us

profile of v5, /device:TPU:1, one launch (start us, length us, event | category | flops | bytes accessed | tf_op | source)
XLA Modules:
  0.0 49.7 jit_solution(2369247437580876211)
XLA Ops:
  0.0 48.4 %shard_map.55 = f32[8,32]{1,0:T(8,128)} custom-call(bf16[32,2048]{1,0:T(8,128)(2,1)} %q_ref.1, s32[1,32]{1,0:T(1,128)} %bitcast.5, s32[2,32]{1,0:T(2,128)} %bitcast.4, s32[8]{0:T(128)} %shifts_ref.1, bf16[128,2048]{1,0:T(8,128)(2,1)} %lib_ref.1), custom_call_target="tpu_custom_call" | custom-call | tf_op jit(solution)/shard_map/pallas_call | solution.py:391
  48.4 1.3 %copy.7 = f32[32,8]{0,1:T(8,128)} copy(f32[32,8]{0,1:T(8,128)} %bitcast.3) | data formatting | bytes 2048
